TPU v7x, 32 devices: a whole 2x2x4 slice. The times are simulated.
32 devices in a mesh: row: 2 (over y), col: 8 (over z, x), leaf: 2 (over core).
Axes of the slice: x: 2, y: 2, z: 4, core: 2. Of those that a mesh axis runs over, the one named last changes fastest.
Arguments:
- front: float32 [4096, 8192], P('row', ('col', 'leaf')), may hold values from -6 to 6
- child: float32 [4096, 8192], P(('row', 'col', 'leaf')), may hold values from -6 to 6
- row_map: int32 [2, 8], P('row'), may hold values from 0 to 7, each once within a row
- col_map: int32 [32], replicated, may hold values from 0 to 31, each once
- x_fac: float32 [16, 16384], P('row', ('col', 'leaf')), may hold values from -0.75 to 0.75
- w_fac: float32 [16, 16384], P('row', ('col', 'leaf')), may hold values from -0.375 to 0.375
- v_fac: float32 [32, 16384], P(('col', 'leaf'), 'row'), may hold values from -6 to 6
- z_fac: float32 [32, 16384], P(('col', 'leaf'), 'row'), may hold values from -0.75 to 0.75
- dinv: float32 [256, 256], replicated, may hold values from -0.375 to 0.375
- pivots: int32 [256], replicated, may hold values from 0 to 255, each once
- rank_rows: int32 [16], P('row'), may hold values from 16 to 64
- rank_cols: int32 [32], P(('col', 'leaf')), may hold values from 16 to 64
- admissible: int32 [16, 32], P('row', ('col', 'leaf')), may hold values 0 or 1
Outputs:
- updated: float32 [4096, 8192], P('row', ('col', 'leaf'))
Inputs may be any that keep to these rules, and one draw needn't show every extreme that they name: Each row of row_map orders the 8 tile rows of one group; col_map orders all 32 tile columns. `pivots`: A permutation of the panel's columns.
All inputs are finite; a program needn't handle non-finite values. No bound on the sum of `admissible` on one device may be relied on, other than what follows from the above.
Results may differ from a plain program's by a relative error of at most 0.0003.
Values sent between devices are 32-bit elements; how exact they have to be, the bound alone decides.
No kernel may reach another device: no remote copies, remote signals or barrier semaphores. Data moves between devices by JAX's collectives and lax.ppermute only.
A program may use at most 128 MiB of HBM per device.

v0:
```python
import functools

import jax
import jax.numpy as jnp
import numpy as np
from jax import lax
from jax.experimental import pallas as pl
from jax.experimental.pallas import tpu as pltpu
from jax.sharding import PartitionSpec as P

RMAX = 64
LANES = 128
NEAR = 4
GROUP = ("col", "leaf")
HIGHEST = lax.Precision.HIGHEST
MIB = 1 << 20


def group_index():
    return lax.axis_index("col") * lax.axis_size("leaf") + lax.axis_index("leaf")


def in_hbm(array):
    return pltpu.with_memory_space_constraint(array, pltpu.HBM)


def place_kernel(tiles, tile, col_map, child, placed, held, in_sem, out_sem):
    def fetch(b):
        return pltpu.make_async_copy(child.at[:, pl.ds(b * tile, tile)], held.at[b], in_sem.at[b])

    def store(b):
        return pltpu.make_async_copy(held.at[b], placed.at[col_map[b]], out_sem.at[b])

    for b in range(tiles):
        fetch(b).start()
    for b in range(tiles):
        fetch(b).wait()
        store(b).start()
    for b in range(tiles):
        store(b).wait()


def place(child, col_map, tile):
    rows = child.shape[0]
    tiles = col_map.shape[0]
    return pl.pallas_call(
        functools.partial(place_kernel, tiles, tile),
        out_shape=pltpu.HBM((tiles, rows, tile), child.dtype),
        in_specs=[pl.BlockSpec(memory_space=pltpu.SMEM), pl.BlockSpec(memory_space=pltpu.HBM)],
        out_specs=pl.BlockSpec(memory_space=pltpu.HBM),
        scratch_shapes=[
            pltpu.VMEM((tiles, rows, tile), child.dtype),
            pltpu.SemaphoreType.DMA((tiles,)),
            pltpu.SemaphoreType.DMA((tiles,)),
        ],
        compiler_params=pltpu.CompilerParams(vmem_limit_bytes=16 * MIB),
        cost_estimate=pl.CostEstimate(flops=0, bytes_accessed=2 * child.size * 4, transcendentals=0),
        name="place_child",
    )(col_map, in_hbm(child))


def dot(a, b, contract=((1,), (0,))):
    return lax.dot_general(a, b, (contract, ((), ())), precision=HIGHEST, preferred_element_type=jnp.float32)


def update_kernel(
    parts, halves, per, row_tiles, col_tiles, tile,
    front, dinv, pivots, keep, *rest,
):
    xw = rest[:parts]
    vz = rest[parts : parts + halves]
    out, xs, ts, vs, zs = rest[parts + halves :]
    step = pl.program_id(0)
    chunk = vz[0].shape[1] // tile
    slots = xw[0].shape[0]
    rows = slots * row_tiles

    @pl.when(step == 0)
    def _():
        hot = (lax.broadcasted_iota(jnp.int32, (tile, tile), 0) == pivots[...]).astype(jnp.float32)
        turned = dot(hot, dinv[...])
        zs[...] = jnp.zeros_like(zs)
        for h in range(halves):
            for j in range(col_tiles):
                for p in range(chunk):
                    r = j * RMAX + h * chunk + p
                    span = pl.ds(p * tile, tile)
                    vs[pl.ds(r, 1), :] = vz[h][pl.ds(j, 1), span]
                    zs[pl.ds(r, 1), pl.ds(j * tile, tile)] = vz[h][pl.ds(col_tiles + j, 1), span]
        dv = dot(turned, vs[...], ((1,), (1,)))
        for q in range(per):
            span = pl.ds(q * tile, tile)
            for n in range(parts):
                at = pl.ds((q * parts + n) * rows, rows)
                left = xw[n][:, :row_tiles, span].reshape(rows, tile)
                for g in range(tile // LANES):
                    xs[g, at, :] = left[:, g * LANES : (g + 1) * LANES]
                core = dot(xw[n][:, row_tiles:, span].reshape(rows, tile), dv)
                kept = jnp.where(keep[at, :] > 0, core, 0.0)
                right = dot(kept, zs[...])
                for g in range(right.shape[1] // LANES):
                    ts[g, at, :] = right[:, g * LANES : (g + 1) * LANES]

    mine = pl.ds(step, RMAX, stride=row_tiles)
    left = jnp.concatenate([xs[g, mine, :] for g in range(xs.shape[0])], axis=1)
    right = jnp.concatenate([ts[g, mine, :] for g in range(ts.shape[0])], axis=1)
    out[...] = front[...] - dot(left, right, ((0,), (0,)))


def subtract_update(front, dinv, pivots, keep, xw, vz):
    tile = dinv.shape[0]
    row_tiles = front.shape[0] // tile
    width = front.shape[1]
    col_tiles = width // tile
    per = xw[0].shape[2] // tile
    total = RMAX * row_tiles

    def whole(array):
        return pl.BlockSpec(array.shape, lambda i: (0,) * array.ndim)

    block = pl.BlockSpec((tile, width), lambda i: (i, 0))
    pivots = pivots.reshape(1, tile)
    return pl.pallas_call(
        functools.partial(update_kernel, len(xw), len(vz), per, row_tiles, col_tiles, tile),
        grid=(row_tiles,),
        out_shape=pltpu.HBM(front.shape, front.dtype),
        in_specs=[block, whole(dinv), whole(pivots), whole(keep)] + [whole(a) for a in xw] + [whole(a) for a in vz],
        out_specs=block,
        scratch_shapes=[
            pltpu.VMEM((tile // LANES, total, LANES), jnp.float32),
            pltpu.VMEM((width // LANES, total, LANES), jnp.float32),
            pltpu.VMEM((col_tiles * RMAX, tile), jnp.float32),
            pltpu.VMEM((col_tiles * RMAX, width), jnp.float32),
        ],
        compiler_params=pltpu.CompilerParams(vmem_limit_bytes=24 * MIB),
        cost_estimate=pl.CostEstimate(flops=2 * front.size * 256, bytes_accessed=2 * front.size * 4, transcendentals=0),
        name="front_less_update",
    )(in_hbm(front), dinv, pivots, keep, *xw, *vz)


def add_kernel(row_tiles, pieces, col_tiles, rows, tile, row_map, base, arrived, out, held, got, base_sem, got_sem, out_sem):
    def at(a):
        return pl.ds(row_map[0, a] * tile, tile)

    def fetch_base(a):
        return pltpu.make_async_copy(base.at[at(a), :], held.at[a], base_sem.at[a])

    def fetch_got(a):
        return pltpu.make_async_copy(arrived.at[pl.ds(a * pieces, pieces)], got.at[a], got_sem.at[a])

    def store(a):
        return pltpu.make_async_copy(held.at[a], out.at[at(a), :], out_sem.at[a])

    for a in range(row_tiles):
        fetch_base(a).start()
        fetch_got(a).start()
    for a in range(row_tiles):
        fetch_base(a).wait()
        fetch_got(a).wait()
        for p in range(pieces):
            for j in range(col_tiles):
                low, left = pl.ds(p * rows, rows), pl.ds(j * tile, tile)
                held[a, low, left] = held[a, low, left] + got[a, p, j]
        store(a).start()
    for a in range(row_tiles):
        store(a).wait()


def add_child(base, arrived, row_map, tile):
    row_tiles = base.shape[0] // tile
    count, col_tiles, rows, _ = arrived.shape
    pieces = count // row_tiles
    return pl.pallas_call(
        functools.partial(add_kernel, row_tiles, pieces, col_tiles, rows, tile),
        out_shape=pltpu.HBM(base.shape, base.dtype),
        in_specs=[
            pl.BlockSpec(memory_space=pltpu.SMEM),
            pl.BlockSpec(memory_space=pltpu.HBM),
            pl.BlockSpec(memory_space=pltpu.HBM),
        ],
        out_specs=pl.BlockSpec(memory_space=pltpu.HBM),
        scratch_shapes=[
            pltpu.VMEM((row_tiles, tile, base.shape[1]), base.dtype),
            pltpu.VMEM((row_tiles, pieces, col_tiles, rows, tile), base.dtype),
            pltpu.SemaphoreType.DMA((row_tiles,)),
            pltpu.SemaphoreType.DMA((row_tiles,)),
            pltpu.SemaphoreType.DMA((row_tiles,)),
        ],
        compiler_params=pltpu.CompilerParams(vmem_limit_bytes=24 * MIB),
        cost_estimate=pl.CostEstimate(flops=base.size, bytes_accessed=3 * base.size * 4, transcendentals=0),
        name="add_child",
    )(row_map, in_hbm(base), in_hbm(arrived))


def swap(array, m):
    size = lax.axis_size("col") * lax.axis_size("leaf")
    return lax.ppermute(array, GROUP, [(d, d ^ m) for d in range(size)])


def gather_row(array):
    size = lax.axis_size("row")
    return [array] + [lax.ppermute(array, "row", [(y, y ^ m) for y in range(size)]) for m in range(1, size)]


def on_device(
    front,
    child,
    row_map,
    col_map,
    x_fac,
    w_fac,
    v_fac,
    z_fac,
    dinv,
    pivots,
    rank_rows,
    rank_cols,
    admissible,
):
    tile = dinv.shape[0]
    row_tiles = front.shape[0] // tile
    col_tiles = front.shape[1] // tile
    devices = lax.axis_size("col") * lax.axis_size("leaf")
    per = x_fac.shape[1] // tile
    chunk = v_fac.shape[1] // tile

    vz = gather_row(jnp.concatenate([v_fac, z_fac], axis=0))
    mine = jnp.concatenate([x_fac, w_fac], axis=0)
    line = [mine] + [swap(mine, m) for m in range(NEAR, devices, NEAR)]
    placed = place(child, col_map, tile).reshape(devices, col_tiles, child.shape[0], tile)
    line, vz, placed = lax.optimization_barrier((line, vz, placed))
    line = jnp.stack(line)
    xw = [line] + [swap(line, m) for m in range(1, NEAR)]
    arrived = lax.all_to_all(placed, GROUP, split_axis=0, concat_axis=0, tiled=True)

    far = np.arange(0, devices, NEAR, dtype=np.int32)
    source = group_index() ^ (far + np.arange(NEAR, dtype=np.int32)[:, None])
    r = source * per + np.arange(per, dtype=np.int32)[:, None, None]
    source = lax.axis_index("row") ^ np.arange(lax.axis_size("row"), dtype=np.int32)
    s = source[:, None] * chunk + np.arange(chunk, dtype=np.int32)
    keep_rows = r.reshape(RMAX, 1) < rank_rows[None, :]
    keep_cols = s.reshape(1, RMAX) < rank_cols[:, None]
    dense = (admissible == 0)[None, :, :, None]
    keep = (keep_rows[:, :, None, None] & keep_cols[None, None]) | dense
    keep = keep.astype(jnp.float32).reshape(RMAX * row_tiles, col_tiles * RMAX)

    base = subtract_update(front, dinv, pivots, keep, xw, vz)
    return add_child(base, arrived, row_map, tile)


def solution(mesh):
    return jax.shard_map(
        on_device,
        mesh=mesh,
        in_specs=(
            P("row", GROUP),
            P(("row", "col", "leaf"), None),
            P("row", None),
            P(),
            P("row", GROUP),
            P("row", GROUP),
            P(GROUP, "row"),
            P(GROUP, "row"),
            P(),
            P(),
            P("row"),
            P(GROUP),
            P("row", GROUP),
        ),
        out_specs=P("row", GROUP),
        check_vma=False,
    )
```

profile of v0, /device:TPU:11, one launch (start us, length us, event | category | flops | bytes accessed | tf_op | source)
XLA Modules:
  0.0 119.5 jit_solution(5686446791872072140)
XLA Ops:
  0.0 0.9 pad_maximum_fusion.1.rest_4_
  0.9 1.3 %collective-permute-start.3 = (f32[4,8192]{1,0:T(4,128)S(1)}, f32[4,8192]{1,0:T(4,128)S(1)}, u32[]{:S(2)}, u32[]{:S(2)}) collective-permute-start(f32[4,8192]{1,0:T(4,128)S(1)} %pad_maximum_fusion.1.rest_4_), channel_id=1, source_target_pairs={{0,16},{16,0},{1,17},{17,1},{2,18},{18,2},{3,19},{19,3},{4,20},{20... | collective-permute-start | bytes 393224 | tf_op jit(solution)/shard_map/ppermute | solution.py:202
  2.2 0.8 constant_dynamic-update-slice_fusion.1
  3.0 0.8 constant_dynamic-update-slice_fusion
  3.8 1.3 %collective-permute-start.2 = (f32[16,1024]{1,0:T(8,128)S(1)}, f32[16,1024]{1,0:T(8,128)S(1)}, u32[]{:S(2)}, u32[]{:S(2)}) collective-permute-start(f32[16,1024]{1,0:T(8,128)S(1)} %constant_dynamic-update-slice_fusion), channel_id=1, source_target_pairs={{0,12},{1,13},{2,14},{3,15},{4,8},{5,9},{6,10},{7,11},{8,4},{9,5},... | collective-permute-start | bytes 196616 | tf_op jit(solution)/shard_map/ppermute | solution.py:197
  5.1 1.0 collective-permute-start.1
  6.1 1.2 collective-permute-start
  7.3 0.0 copy-start.2
  7.3 0.7 copy-done.2
  7.9 5.2 %place_child.1 = f32[32,128,256]{2,1,0:T(8,128)} custom-call(s32[32]{0:T(128)S(1)} %copy-done.2, f32[128,8192]{1,0:T(8,128)} %child.1), custom_call_target="tpu_custom_call" | custom-call | bytes 8388608 | tf_op jit(solution)/shard_map/place_child/pallas_call | solution.py:46
  13.1 0.0 collective-permute-done.2
  13.1 0.0 collective-permute-done.1
  13.1 0.0 collective-permute-done
  13.1 0.0 collective-permute-done.3.rest_5_
  13.1 0.0 copy-start.6
  13.1 0.0 copy-start.4
  13.1 0.0 copy-start.7
  13.2 0.0 copy-start.5
  13.2 0.0 copy-start
  13.2 0.0 copy-start.1
  13.2 7.9 %all-to-all-start = ((f32[16,2,128,256]{3,2,1,0:T(8,128)}), f32[16,2,128,256]{3,2,1,0:T(8,128)}, u32[]{:S(2)}, u32[]{:S(2)}) async-start(f32[16,2,128,256]{3,2,1,0:T(8,128)} %bitcast.11), calls=%async_computation | async-start | bytes 8388608 | tf_op jit(solution)/shard_map/all_to_all | solution.py:234
  21.1 0.0 copy-done.6
  21.1 0.0 copy-done.4
  21.2 0.6 collective-permute-start.6
  21.8 1.2 collective-permute-start.5
  22.9 0.4 collective-permute-start.4
  23.4 0.1 iota_add_fusion.1
  23.5 0.1 copy.19
  23.5 0.1 add.54
  23.6 0.1 lt.48
  23.7 0.0 copy-done.7
  23.7 0.1 lt.49
  23.8 0.1 lt.50
  23.9 0.1 add.50
  24.0 0.1 lt.42
  24.0 0.1 lt.43
  24.1 0.0 copy-done.5
  24.2 0.1 lt.45
  24.3 0.2 or.11
  24.5 0.2 or.12
  24.7 0.1 or_convert_fusion.keep
  24.9 26.2 %collective-permute-done.6.rest_3_ = f32[4,16,1024]{2,1,0:T(8,128)S(1)} collective-permute-done((f32[4,16,1024]{2,1,0:T(8,128)S(1)}, f32[4,16,1024]{2,1,0:T(8,128)S(1)}, u32[]{:S(2)}, u32[]{:S(2)}) %collective-permute-start.6) | collective-permute-done | bytes 262176 | tf_op jit(solution)/shard_map/ppermute | solution.py:197
  51.1 5.0 %collective-permute-done.5.rest_2_ = f32[4,16,1024]{2,1,0:T(8,128)S(1)} collective-permute-done((f32[4,16,1024]{2,1,0:T(8,128)S(1)}, f32[4,16,1024]{2,1,0:T(8,128)S(1)}, u32[]{:S(2)}, u32[]{:S(2)}) %collective-permute-start.5) | collective-permute-done | bytes 262176 | tf_op jit(solution)/shard_map/ppermute | solution.py:197
  56.0 0.0 collective-permute-done.4.rest_1_
  56.0 0.0 copy-done
  56.0 0.0 copy-done.1
  56.0 0.0 copy-start.3
  56.0 14.4 %front_less_update.1.base = f32[2048,512]{1,0:T(8,128)} custom-call(f32[2048,512]{1,0:T(8,128)} %front.1, f32[256,256]{1,0:T(8,128)S(1)} %copy-done, s32[1,256]{1,0:T(1,128)S(1)} %bitcast.10, f32[512,128]{1,0:T(8,128)S(1)} %or_convert_fusion.keep, f32[4,16,1024]{2,1,0:T(8,128)S(1)} %pad_maximum_fusion.rest_0_, ...), custom_call_target="tpu_custom_call" | custom-call | flops 536870912 | bytes 8388608 | tf_op jit(solution)/shard_map/front_less_update/pallas_call | solution.py:123
  70.4 43.2 %all-to-all-done.arrived = f32[16,2,128,256]{3,2,1,0:T(8,128)} async-done(((f32[16,2,128,256]{3,2,1,0:T(8,128)}), f32[16,2,128,256]{3,2,1,0:T(8,128)}, u32[]{:S(2)}, u32[]{:S(2)}) %all-to-all-start) | async-done | bytes 4194336 | tf_op jit(solution)/shard_map/all_to_all | solution.py:234
  113.6 0.0 copy-done.3
  113.6 5.9 %add_child.1 = f32[2048,512]{1,0:T(8,128)} custom-call(s32[1,8]{1,0:T(1,128)S(1)} %copy-done.3, f32[2048,512]{1,0:T(8,128)} %front_less_update.1.base, f32[16,2,128,256]{3,2,1,0:T(8,128)} %all-to-all-done.arrived), custom_call_target="tpu_custom_call" | custom-call | flops 1048576 | bytes 12582912 | tf_op jit(solution)/shard_map/add_child/pallas_call | solution.py:173
  (9 shorter events, 0.1 us)
Async XLA Ops:
  0.9 12.2 %collective-permute-start.3 = (f32[4,8192]{1,0:T(4,128)S(1)}, f32[4,8192]{1,0:T(4,128)S(1)}, u32[]{:S(2)}, u32[]{:S(2)}) collective-permute-start(f32[4,8192]{1,0:T(4,128)S(1)} %pad_maximum_fusion.1.rest_4_), channel_id=1, source_target_pairs={{0,16},{16,0},{1,17},{17,1},{2,18},{18,2},{3,19},{19,3},{4,20},{20... | collective-permute-start | bytes 393224 | tf_op jit(solution)/shard_map/ppermute | solution.py:202
  3.8 9.3 %collective-permute-start.2 = (f32[16,1024]{1,0:T(8,128)S(1)}, f32[16,1024]{1,0:T(8,128)S(1)}, u32[]{:S(2)}, u32[]{:S(2)}) collective-permute-start(f32[16,1024]{1,0:T(8,128)S(1)} %constant_dynamic-update-slice_fusion), channel_id=1, source_target_pairs={{0,12},{1,13},{2,14},{3,15},{4,8},{5,9},{6,10},{7,11},{8,4},{9,5},... | collective-permute-start | bytes 196616 | tf_op jit(solution)/shard_map/ppermute | solution.py:197
  5.1 8.0 %collective-permute-start.1 = (f32[16,1024]{1,0:T(8,128)S(1)}, f32[16,1024]{1,0:T(8,128)S(1)}, u32[]{:S(2)}, u32[]{:S(2)}) collective-permute-start(f32[16,1024]{1,0:T(8,128)S(1)} %constant_dynamic-update-slice_fusion), channel_id=1, source_target_pairs={{0,8},{1,9},{2,10},{3,11},{4,12},{5,13},{6,14},{7,15},{8,0},{9,1},... | collective-permute-start | bytes 196616 | tf_op jit(solution)/shard_map/ppermute | solution.py:197
  6.1 7.0 %collective-permute-start = (f32[16,1024]{1,0:T(8,128)S(1)}, f32[16,1024]{1,0:T(8,128)S(1)}, u32[]{:S(2)}, u32[]{:S(2)}) collective-permute-start(f32[16,1024]{1,0:T(8,128)S(1)} %constant_dynamic-update-slice_fusion), channel_id=1, source_target_pairs={{0,4},{1,5},{2,6},{3,7},{4,0},{5,1},{6,2},{7,3},{8,12},{9,13},{10,... | collective-permute-start | bytes 196616 | tf_op jit(solution)/shard_map/ppermute | solution.py:197
  7.3 0.7 copy-start.2
  13.1 8.0 %copy-start.6 = (s32[8,2]{0,1:T(2,128)S(1)}, s32[8,2]{0,1:T(2,128)}, u32[]{:S(2)}) copy-start(s32[8,2]{0,1:T(2,128)} %param.29) | copy-start | bytes 196
  13.1 8.0 %copy-start.4 = (s32[4,4]{1,0:T(4,128)S(1)}, s32[4,4]{1,0:T(4,128)}, u32[]{:S(2)}) copy-start(s32[4,4]{1,0:T(4,128)} %constant.28.clone) | copy-start | bytes 196
  13.1 10.6 %copy-start.7 = (s32[2]{0:T(128)S(1)}, s32[2]{0:T(128)}, u32[]{:S(2)}) copy-start(s32[2]{0:T(128)} %param.28) | copy-start | bytes 28
  13.2 11.0 %copy-start.5 = (s32[8]{0:T(128)S(1)}, s32[8]{0:T(128)}, u32[]{:S(2)}) copy-start(s32[8]{0:T(128)} %param.27) | copy-start | bytes 100
  13.2 42.9 %copy-start = (f32[256,256]{1,0:T(8,128)S(1)}, f32[256,256]{1,0:T(8,128)}, u32[]{:S(2)}) copy-start(f32[256,256]{1,0:T(8,128)} %dinv.1) | copy-start | bytes 786436
  13.2 42.9 %copy-start.1 = (s32[256]{0:T(256)S(1)}, s32[256]{0:T(256)}, u32[]{:S(2)}) copy-start(s32[256]{0:T(256)} %param.26) | copy-start | bytes 3076
  13.2 100.4 %all-to-all-start = ((f32[16,2,128,256]{3,2,1,0:T(8,128)}), f32[16,2,128,256]{3,2,1,0:T(8,128)}, u32[]{:S(2)}, u32[]{:S(2)}) async-start(f32[16,2,128,256]{3,2,1,0:T(8,128)} %bitcast.11), calls=%async_computation | async-start | bytes 8388608 | tf_op jit(solution)/shard_map/all_to_all | solution.py:234
  21.2 29.9 %collective-permute-start.6 = (f32[4,16,1024]{2,1,0:T(8,128)S(1)}, f32[4,16,1024]{2,1,0:T(8,128)S(1)}, u32[]{:S(2)}, u32[]{:S(2)}) collective-permute-start(f32[4,16,1024]{2,1,0:T(8,128)S(1)} %pad_maximum_fusion.rest_0_), channel_id=1, source_target_pairs={{0,3},{1,2},{2,1},{3,0},{4,7},{5,6},{6,5},{7,4},{8,11},{9,10},{10,... | collective-permute-start | bytes 786440 | tf_op jit(solution)/shard_map/ppermute | solution.py:197
  21.8 34.3 %collective-permute-start.5 = (f32[4,16,1024]{2,1,0:T(8,128)S(1)}, f32[4,16,1024]{2,1,0:T(8,128)S(1)}, u32[]{:S(2)}, u32[]{:S(2)}) collective-permute-start(f32[4,16,1024]{2,1,0:T(8,128)S(1)} %pad_maximum_fusion.rest_0_), channel_id=1, source_target_pairs={{0,2},{1,3},{2,0},{3,1},{4,6},{5,7},{6,4},{7,5},{8,10},{9,11},{10,... | collective-permute-start | bytes 786440 | tf_op jit(solution)/shard_map/ppermute | solution.py:197
  22.9 33.1 %collective-permute-start.4 = (f32[4,16,1024]{2,1,0:T(8,128)S(1)}, f32[4,16,1024]{2,1,0:T(8,128)S(1)}, u32[]{:S(2)}, u32[]{:S(2)}) collective-permute-start(f32[4,16,1024]{2,1,0:T(8,128)S(1)} %pad_maximum_fusion.rest_0_), channel_id=1, source_target_pairs={{0,1},{1,0},{2,3},{3,2},{4,5},{5,4},{6,7},{7,6},{8,9},{9,8},{10,11... | collective-permute-start | bytes 786440 | tf_op jit(solution)/shard_map/ppermute | solution.py:197
  56.0 57.5 %copy-start.3 = (s32[1,8]{1,0:T(1,128)S(1)}, s32[1,8]{1,0:T(1,128)}, u32[]{:S(2)}) copy-start(s32[1,8]{1,0:T(1,128)} %row_map.1) | copy-start | bytes 100
where the time goes:
time: 120 us; the launch traced here: 119 us
  waiting for transfers between devices  74.4 us (62%)
  Pallas kernels  25.4 us (21%)
  starting transfers between devices  14.9 us (12%)
  local copies, waits for them, and re-layouts  3.41 us (3%)
    all_to_all x1, waiting for transfers between devices, on_device(): lax.all_to_all(placed, GROUP, split_axis=0, concat_axis=0, tiled=True)  43.2 us
    ppermute x6, waiting for transfers between devices, swap(): return lax.ppermute(array, GROUP, [(d, d ^ m) for d in range(size)])  31.2 us
    pallas_call x1, Pallas kernels, subtract_update(): pl.pallas_call(functools.partial(update_kernel, len(xw), len(vz), per, ro...  14.4 us
    all_to_all x1, starting transfers between devices, on_device(): lax.all_to_all(placed, GROUP, split_axis=0, concat_axis=0, tiled=True)  7.87 us
    pallas_call x1, Pallas kernels, add_child(): pl.pallas_call(functools.partial(add_kernel, row_tiles, pieces, col_tiles...  5.92 us
    ppermute x6, starting transfers between devices, swap(): return lax.ppermute(array, GROUP, [(d, d ^ m) for d in range(size)])  5.71 us
    pallas_call x1, Pallas kernels, place(): pl.pallas_call(functools.partial(place_kernel, tiles, tile), out_shape=pl...  5.16 us
  transfers between devices with their start and end apart: 8, of which 3 were waited for; matrix products, arithmetic and copies ran while one was open for 2% of the time, Pallas kernels for 16%

commit v1 on v0

--- a/solution.py
+++ b/solution.py
@@ -24,39 +24,48 @@
     return pltpu.with_memory_space_constraint(array, pltpu.HBM)
 
 
-def place_kernel(tiles, tile, col_map, child, placed, held, in_sem, out_sem):
-    def fetch(b):
-        return pltpu.make_async_copy(child.at[:, pl.ds(b * tile, tile)], held.at[b], in_sem.at[b])
+def place_kernel(tiles, groups, tile, col_map, child, placed, held, in_sem, out_sem):
+    width = tiles // groups * tile
+
+    def fetch(g):
+        span = pl.ds(g * width, width)
+        return pltpu.make_async_copy(child.at[:, span], held.at[:, span], in_sem.at[g])
 
     def store(b):
-        return pltpu.make_async_copy(held.at[b], placed.at[col_map[b]], out_sem.at[b])
-
-    for b in range(tiles):
-        fetch(b).start()
-    for b in range(tiles):
-        fetch(b).wait()
-        store(b).start()
+        return pltpu.make_async_copy(held.at[:, pl.ds(b * tile, tile)], placed.at[col_map[b]], out_sem.at[b])
+
+    for g in range(groups):
+        fetch(g).start()
+    for g in range(groups):
+        fetch(g).wait()
+        for b in range(g * tiles // groups, (g + 1) * tiles // groups):
+            store(b).start()
     for b in range(tiles):
         store(b).wait()
+
+
+def in_vmem(array):
+    return pltpu.with_memory_space_constraint(array, pltpu.VMEM)
 
 
 def place(child, col_map, tile):
     rows = child.shape[0]
     tiles = col_map.shape[0]
+    groups = 8
     return pl.pallas_call(
-        functools.partial(place_kernel, tiles, tile),
+        functools.partial(place_kernel, tiles, groups, tile),
         out_shape=pltpu.HBM((tiles, rows, tile), child.dtype),
         in_specs=[pl.BlockSpec(memory_space=pltpu.SMEM), pl.BlockSpec(memory_space=pltpu.HBM)],
         out_specs=pl.BlockSpec(memory_space=pltpu.HBM),
         scratch_shapes=[
-            pltpu.VMEM((tiles, rows, tile), child.dtype),
-            pltpu.SemaphoreType.DMA((tiles,)),
+            pltpu.VMEM(child.shape, child.dtype),
+            pltpu.SemaphoreType.DMA((groups,)),
             pltpu.SemaphoreType.DMA((tiles,)),
         ],
         compiler_params=pltpu.CompilerParams(vmem_limit_bytes=16 * MIB),
         cost_estimate=pl.CostEstimate(flops=0, bytes_accessed=2 * child.size * 4, transcendentals=0),
         name="place_child",
-    )(col_map, in_hbm(child))
+    )(in_hbm(col_map), in_hbm(child))
 
 
 def dot(a, b, contract=((1,), (0,))):
@@ -123,7 +132,7 @@
     return pl.pallas_call(
         functools.partial(update_kernel, len(xw), len(vz), per, row_tiles, col_tiles, tile),
         grid=(row_tiles,),
-        out_shape=pltpu.HBM(front.shape, front.dtype),
+        out_shape=pltpu.VMEM(front.shape, front.dtype),
         in_specs=[block, whole(dinv), whole(pivots), whole(keep)] + [whole(a) for a in xw] + [whole(a) for a in vz],
         out_specs=block,
         scratch_shapes=[
@@ -138,29 +147,24 @@
     )(in_hbm(front), dinv, pivots, keep, *xw, *vz)
 
 
-def add_kernel(row_tiles, pieces, col_tiles, rows, tile, row_map, base, arrived, out, held, got, base_sem, got_sem, out_sem):
-    def at(a):
-        return pl.ds(row_map[0, a] * tile, tile)
-
-    def fetch_base(a):
-        return pltpu.make_async_copy(base.at[at(a), :], held.at[a], base_sem.at[a])
-
-    def fetch_got(a):
+def add_kernel(row_tiles, pieces, col_tiles, rows, tile, row_map, base, arrived, out, held, got, got_sem, out_sem):
+    def at(a, p):
+        return pl.ds(pl.multiple_of(row_map[0, a] * tile + p * rows, rows), rows)
+
+    def fetch(a):
         return pltpu.make_async_copy(arrived.at[pl.ds(a * pieces, pieces)], got.at[a], got_sem.at[a])
 
     def store(a):
-        return pltpu.make_async_copy(held.at[a], out.at[at(a), :], out_sem.at[a])
+        return pltpu.make_async_copy(held.at[a], out.at[pl.ds(row_map[0, a] * tile, tile), :], out_sem.at[a])
 
     for a in range(row_tiles):
-        fetch_base(a).start()
-        fetch_got(a).start()
+        fetch(a).start()
     for a in range(row_tiles):
-        fetch_base(a).wait()
-        fetch_got(a).wait()
+        fetch(a).wait()
         for p in range(pieces):
             for j in range(col_tiles):
-                low, left = pl.ds(p * rows, rows), pl.ds(j * tile, tile)
-                held[a, low, left] = held[a, low, left] + got[a, p, j]
+                span = pl.ds(j * tile, tile)
+                held[a, pl.ds(p * rows, rows), span] = base[at(a, p), span] + got[a, p, j]
         store(a).start()
     for a in range(row_tiles):
         store(a).wait()
@@ -175,7 +179,7 @@
         out_shape=pltpu.HBM(base.shape, base.dtype),
         in_specs=[
             pl.BlockSpec(memory_space=pltpu.SMEM),
-            pl.BlockSpec(memory_space=pltpu.HBM),
+            pl.BlockSpec(memory_space=pltpu.VMEM),
             pl.BlockSpec(memory_space=pltpu.HBM),
         ],
         out_specs=pl.BlockSpec(memory_space=pltpu.HBM),
@@ -184,12 +188,11 @@
             pltpu.VMEM((row_tiles, pieces, col_tiles, rows, tile), base.dtype),
             pltpu.SemaphoreType.DMA((row_tiles,)),
             pltpu.SemaphoreType.DMA((row_tiles,)),
-            pltpu.SemaphoreType.DMA((row_tiles,)),
         ],
         compiler_params=pltpu.CompilerParams(vmem_limit_bytes=24 * MIB),
         cost_estimate=pl.CostEstimate(flops=base.size, bytes_accessed=3 * base.size * 4, transcendentals=0),
         name="add_child",
-    )(row_map, in_hbm(base), in_hbm(arrived))
+    )(in_hbm(row_map), in_vmem(base), in_hbm(arrived))
 
 
 def swap(array, m):
@@ -224,12 +227,14 @@
     per = x_fac.shape[1] // tile
     chunk = v_fac.shape[1] // tile
 
-    vz = gather_row(jnp.concatenate([v_fac, z_fac], axis=0))
-    mine = jnp.concatenate([x_fac, w_fac], axis=0)
+    mine = jnp.pad(x_fac, ((0, row_tiles), (0, 0))) + jnp.pad(w_fac, ((row_tiles, 0), (0, 0)))
     line = [mine] + [swap(mine, m) for m in range(NEAR, devices, NEAR)]
     placed = place(child, col_map, tile).reshape(devices, col_tiles, child.shape[0], tile)
-    line, vz, placed = lax.optimization_barrier((line, vz, placed))
+    line, placed, v_fac, z_fac, rank_rows, rank_cols, admissible = lax.optimization_barrier(
+        (line, placed, v_fac, z_fac, rank_rows, rank_cols, admissible)
+    )
     line = jnp.stack(line)
+    vz = gather_row(jnp.concatenate([v_fac, z_fac], axis=0))
     xw = [line] + [swap(line, m) for m in range(1, NEAR)]
     arrived = lax.all_to_all(placed, GROUP, split_axis=0, concat_axis=0, tiled=True)
 

time: 120 us -> 116 us (0.967)
  Pallas kernels: 25.4 us -> 21.6 us
  local copies, waits for them, and re-layouts: 3.41 us -> 5.44 us
  waiting for transfers between devices: 74.4 us -> 72.4 us
    ppermute x6, waiting for transfers between devices: 31.2 us -> 26.5 us  [swap(): return lax.ppermute(array, GROUP, [(d, d ^ m) for d in range(size)])]
    ppermute x1, waiting for transfers between devices: 0.01 us -> 3.32 us  [gather_row(): lax.ppermute(array, 'row', [(y, y ^ m) for y in range(size)])]
    unnamed x17 -> x20, local copies, waits for them, and re-layouts: 1.46 us -> 4.25 us
    pallas_call x1, Pallas kernels: 5.92 us -> 4.14 us  [add_child(): pl.pallas_call(functools.partial(add_kernel, row_tiles, pieces, col_tiles...]
    pallas_call x1, Pallas kernels: 14.4 us -> 12.9 us  [subtract_update(): pl.pallas_call(functools.partial(update_kernel, len(xw), len(vz), per, ro...]
  transfers between devices with their start and end apart: 8 -> 8, of which waited for: 3 -> 4; matrix products, arithmetic and copies ran while one was open for 2% -> 1% of each run, Pallas kernels for 16% -> 15%
where the time goes in v1:
time: 116 us; the launch traced here: 115 us
  waiting for transfers between devices  72.4 us (62%)
  Pallas kernels  21.6 us (19%)
  starting transfers between devices  14.6 us (13%)
  local copies, waits for them, and re-layouts  5.44 us (5%)
    all_to_all x1, waiting for transfers between devices, on_device(): lax.all_to_all(placed, GROUP, split_axis=0, concat_axis=0, tiled=True)  42.6 us
    ppermute x6, waiting for transfers between devices, swap(): return lax.ppermute(array, GROUP, [(d, d ^ m) for d in range(size)])  26.5 us
    pallas_call x1, Pallas kernels, subtract_update(): pl.pallas_call(functools.partial(update_kernel, len(xw), len(vz), per, ro...  12.9 us
    all_to_all x1, starting transfers between devices, on_device(): lax.all_to_all(placed, GROUP, split_axis=0, concat_axis=0, tiled=True)  7.59 us
    ppermute x6, starting transfers between devices, swap(): return lax.ppermute(array, GROUP, [(d, d ^ m) for d in range(size)])  5.71 us
    pallas_call x1, Pallas kernels, place(): pl.pallas_call(functools.partial(place_kernel, tiles, groups, tile), out_...  4.52 us
    unnamed x20, local copies, waits for them, and re-layouts  4.25 us
    pallas_call x1, Pallas kernels, add_child(): pl.pallas_call(functools.partial(add_kernel, row_tiles, pieces, col_tiles...  4.14 us
  transfers between devices with their start and end apart: 8, of which 4 were waited for; matrix products, arithmetic and copies ran while one was open for 1% of the time, Pallas kernels for 15%

profile of v1, /device:TPU:11, one launch (start us, length us, event | category | flops | bytes accessed | tf_op | source)
XLA Modules:
  0.0 115.4 jit_solution(13236585722035757763)
XLA Ops:
  0.0 0.8 pad_add_fusion
  0.8 1.3 %collective-permute-start.2 = (f32[16,1024]{1,0:T(8,128)S(1)}, f32[16,1024]{1,0:T(8,128)S(1)}, u32[]{:S(2)}, u32[]{:S(2)}) collective-permute-start(f32[16,1024]{1,0:T(8,128)S(1)} %pad_add_fusion), channel_id=1, source_target_pairs={{0,12},{1,13},{2,14},{3,15},{4,8},{5,9},{6,10},{7,11},{8,4},{9,5},... | collective-permute-start | bytes 196616 | tf_op jit(solution)/shard_map/ppermute | solution.py:200
  2.1 1.1 collective-permute-start.1
  3.2 1.1 collective-permute-start
  4.3 4.5 %place_child.1 = f32[32,128,256]{2,1,0:T(8,128)} custom-call(s32[32]{0:T(128)} %col_map.1, f32[128,8192]{1,0:T(8,128)} %child.1), custom_call_target="tpu_custom_call" | custom-call | bytes 8388608 | tf_op jit(solution)/shard_map/place_child/pallas_call | solution.py:55
  8.8 0.0 collective-permute-done.2
  8.8 0.0 collective-permute-done.1
  8.8 0.0 collective-permute-done
  8.8 0.0 copy-start.6
  8.8 0.0 copy-start.4
  8.9 0.0 copy-start.5
  8.9 0.0 copy-start.8
  8.9 0.0 copy-start.9
  8.9 0.0 copy-start.7
  8.9 0.0 copy-start.2
  8.9 0.0 copy-start.3
  8.9 7.6 %all-to-all-start = ((f32[16,2,128,256]{3,2,1,0:T(8,128)}), f32[16,2,128,256]{3,2,1,0:T(8,128)}, u32[]{:S(2)}, u32[]{:S(2)}) async-start(f32[16,2,128,256]{3,2,1,0:T(8,128)} %bitcast.11), calls=%async_computation | async-start | bytes 8388608 | tf_op jit(solution)/shard_map/all_to_all | solution.py:239
  16.5 0.1 iota_add_fusion.1
  16.6 0.1 add.62
  16.7 0.1 lt.48
  16.8 0.0 copy-done.6
  16.8 0.1 add.57
  16.9 0.1 lt.42
  17.0 0.1 lt.43
  17.1 0.6 collective-permute-start.5
  17.7 1.2 %collective-permute-start.4 = (f32[4,16,1024]{2,1,0:T(8,128)S(1)}, f32[4,16,1024]{2,1,0:T(8,128)S(1)}, u32[]{:S(2)}, u32[]{:S(2)}) collective-permute-start(f32[4,16,1024]{2,1,0:T(8,128)S(1)} %pad_maximum_fusion.rest_0_), channel_id=1, source_target_pairs={{0,2},{1,3},{2,0},{3,1},{4,6},{5,7},{6,4},{7,5},{8,10},{9,11},{10,... | collective-permute-start | bytes 786440 | tf_op jit(solution)/shard_map/ppermute | solution.py:200
  18.9 0.4 collective-permute-start.3
  19.3 0.0 copy-done.4
  19.3 0.0 copy-done.5
  19.3 0.1 pad_maximum_fusion.1.rest_4_
  19.4 0.0 copy-done.8
  19.4 0.1 copy.19
  19.5 0.0 copy-done.9
  19.5 0.1 lt.49
  19.6 0.1 lt.50
  19.7 0.0 copy-done.7
  19.7 0.1 lt.45
  19.8 1.3 %collective-permute-start.6 = (f32[4,8192]{1,0:T(4,128)S(1)}, f32[4,8192]{1,0:T(4,128)S(1)}, u32[]{:S(2)}, u32[]{:S(2)}) collective-permute-start(f32[4,8192]{1,0:T(4,128)S(1)} %pad_maximum_fusion.1.rest_4_), channel_id=1, source_target_pairs={{0,16},{16,0},{1,17},{17,1},{2,18},{18,2},{3,19},{19,3},{4,20},{20... | collective-permute-start | bytes 393224 | tf_op jit(solution)/shard_map/ppermute | solution.py:205
  21.1 0.2 or.11
  21.3 0.2 or.12
  21.5 0.1 or_convert_fusion.keep
  21.7 3.3 %collective-permute-done.6.rest_5_ = f32[4,8192]{1,0:T(4,128)S(1)} collective-permute-done((f32[4,8192]{1,0:T(4,128)S(1)}, f32[4,8192]{1,0:T(4,128)S(1)}, u32[]{:S(2)}, u32[]{:S(2)}) %collective-permute-start.6) | collective-permute-done | bytes 131104 | tf_op jit(solution)/shard_map/ppermute | solution.py:205
  25.0 21.5 %collective-permute-done.5.rest_3_ = f32[4,16,1024]{2,1,0:T(8,128)S(1)} collective-permute-done((f32[4,16,1024]{2,1,0:T(8,128)S(1)}, f32[4,16,1024]{2,1,0:T(8,128)S(1)}, u32[]{:S(2)}, u32[]{:S(2)}) %collective-permute-start.5) | collective-permute-done | bytes 262176 | tf_op jit(solution)/shard_map/ppermute | solution.py:200
  46.5 5.0 %collective-permute-done.4.rest_2_ = f32[4,16,1024]{2,1,0:T(8,128)S(1)} collective-permute-done((f32[4,16,1024]{2,1,0:T(8,128)S(1)}, f32[4,16,1024]{2,1,0:T(8,128)S(1)}, u32[]{:S(2)}, u32[]{:S(2)}) %collective-permute-start.4) | collective-permute-done | bytes 262176 | tf_op jit(solution)/shard_map/ppermute | solution.py:200
  51.5 0.0 collective-permute-done.3.rest_1_
  51.5 0.0 copy-done.2
  51.5 0.0 copy-done.3
  51.5 12.9 %front_less_update.1.base = f32[2048,512]{1,0:T(8,128)S(1)} custom-call(f32[2048,512]{1,0:T(8,128)} %front.1, f32[256,256]{1,0:T(8,128)S(1)} %copy-done.2, s32[1,256]{1,0:T(1,128)S(1)} %bitcast.10, f32[512,128]{1,0:T(8,128)S(1)} %or_convert_fusion.keep, f32[4,16,1024]{2,1,0:T(8,128)S(1)} %pad_maximum_fusion.rest_0_, ...), custom_call_target="tpu_custom_call" | custom-call | flops 536870912 | bytes 8388608 | tf_op jit(solution)/shard_map/front_less_update/pallas_call | solution.py:132
  64.4 0.0 copy-start
  64.5 2.0 %copy-done = f32[2048,512]{1,0:T(8,128)} copy-done((f32[2048,512]{1,0:T(8,128)}, f32[2048,512]{1,0:T(8,128)S(1)}, u32[]{:S(2)}) %copy-start) | copy-done | bytes 4194328
  66.5 42.6 %all-to-all-done.arrived = f32[16,2,128,256]{3,2,1,0:T(8,128)} async-done(((f32[16,2,128,256]{3,2,1,0:T(8,128)}), f32[16,2,128,256]{3,2,1,0:T(8,128)}, u32[]{:S(2)}, u32[]{:S(2)}) %all-to-all-start) | async-done | bytes 4194336 | tf_op jit(solution)/shard_map/all_to_all | solution.py:239
  109.0 0.0 copy-start.1
  109.0 2.2 %copy-done.1 = f32[2048,512]{1,0:T(8,128)S(1)} copy-done((f32[2048,512]{1,0:T(8,128)S(1)}, f32[2048,512]{1,0:T(8,128)}, u32[]{:S(2)}) %copy-start.1) | copy-done | bytes 4194328
  111.2 4.1 %add_child.1 = f32[2048,512]{1,0:T(8,128)} custom-call(s32[1,8]{1,0:T(1,128)} %row_map.1, f32[2048,512]{1,0:T(8,128)S(1)} %copy-done.1, f32[16,2,128,256]{3,2,1,0:T(8,128)} %all-to-all-done.arrived), custom_call_target="tpu_custom_call" | custom-call | flops 1048576 | bytes 12582912 | tf_op jit(solution)/shard_map/add_child/pallas_call | solution.py:177
  (9 shorter events, 0.1 us)
Async XLA Ops:
  0.8 8.0 %collective-permute-start.2 = (f32[16,1024]{1,0:T(8,128)S(1)}, f32[16,1024]{1,0:T(8,128)S(1)}, u32[]{:S(2)}, u32[]{:S(2)}) collective-permute-start(f32[16,1024]{1,0:T(8,128)S(1)} %pad_add_fusion), channel_id=1, source_target_pairs={{0,12},{1,13},{2,14},{3,15},{4,8},{5,9},{6,10},{7,11},{8,4},{9,5},... | collective-permute-start | bytes 196616 | tf_op jit(solution)/shard_map/ppermute | solution.py:200
  2.1 6.7 %collective-permute-start.1 = (f32[16,1024]{1,0:T(8,128)S(1)}, f32[16,1024]{1,0:T(8,128)S(1)}, u32[]{:S(2)}, u32[]{:S(2)}) collective-permute-start(f32[16,1024]{1,0:T(8,128)S(1)} %pad_add_fusion), channel_id=1, source_target_pairs={{0,8},{1,9},{2,10},{3,11},{4,12},{5,13},{6,14},{7,15},{8,0},{9,1},... | collective-permute-start | bytes 196616 | tf_op jit(solution)/shard_map/ppermute | solution.py:200
  3.2 5.7 %collective-permute-start = (f32[16,1024]{1,0:T(8,128)S(1)}, f32[16,1024]{1,0:T(8,128)S(1)}, u32[]{:S(2)}, u32[]{:S(2)}) collective-permute-start(f32[16,1024]{1,0:T(8,128)S(1)} %pad_add_fusion), channel_id=1, source_target_pairs={{0,4},{1,5},{2,6},{3,7},{4,0},{5,1},{6,2},{7,3},{8,12},{9,13},{10,... | collective-permute-start | bytes 196616 | tf_op jit(solution)/shard_map/ppermute | solution.py:200
  8.8 7.9 %copy-start.6 = (s32[4,4]{1,0:T(4,128)S(1)}, s32[4,4]{1,0:T(4,128)}, u32[]{:S(2)}) copy-start(s32[4,4]{1,0:T(4,128)} %constant.31.clone) | copy-start | bytes 196
  8.8 10.5 %copy-start.4 = (f32[2,8192]{1,0:T(2,128)S(1)}, f32[2,8192]{1,0:T(2,128)}, u32[]{:S(2)}) copy-start(f32[2,8192]{1,0:T(2,128)} %param.24) | copy-start | bytes 196612
  8.9 10.5 %copy-start.5 = (f32[2,8192]{1,0:T(2,128)S(1)}, f32[2,8192]{1,0:T(2,128)}, u32[]{:S(2)}) copy-start(f32[2,8192]{1,0:T(2,128)} %param.23) | copy-start | bytes 196612
  8.9 10.5 %copy-start.8 = (s32[8,2]{0,1:T(2,128)S(1)}, s32[8,2]{0,1:T(2,128)}, u32[]{:S(2)}) copy-start(s32[8,2]{0,1:T(2,128)} %param.29) | copy-start | bytes 196
  8.9 10.6 %copy-start.9 = (s32[2]{0:T(128)S(1)}, s32[2]{0:T(128)}, u32[]{:S(2)}) copy-start(s32[2]{0:T(128)} %param.28) | copy-start | bytes 28
  8.9 10.8 %copy-start.7 = (s32[8]{0:T(128)S(1)}, s32[8]{0:T(128)}, u32[]{:S(2)}) copy-start(s32[8]{0:T(128)} %param.27) | copy-start | bytes 100
  8.9 42.6 %copy-start.2 = (f32[256,256]{1,0:T(8,128)S(1)}, f32[256,256]{1,0:T(8,128)}, u32[]{:S(2)}) copy-start(f32[256,256]{1,0:T(8,128)} %dinv.1) | copy-start | bytes 786436
  8.9 42.6 %copy-start.3 = (s32[256]{0:T(256)S(1)}, s32[256]{0:T(256)}, u32[]{:S(2)}) copy-start(s32[256]{0:T(256)} %param.26) | copy-start | bytes 3076
  8.9 100.1 %all-to-all-start = ((f32[16,2,128,256]{3,2,1,0:T(8,128)}), f32[16,2,128,256]{3,2,1,0:T(8,128)}, u32[]{:S(2)}, u32[]{:S(2)}) async-start(f32[16,2,128,256]{3,2,1,0:T(8,128)} %bitcast.11), calls=%async_computation | async-start | bytes 8388608 | tf_op jit(solution)/shard_map/all_to_all | solution.py:239
  17.1 29.4 %collective-permute-start.5 = (f32[4,16,1024]{2,1,0:T(8,128)S(1)}, f32[4,16,1024]{2,1,0:T(8,128)S(1)}, u32[]{:S(2)}, u32[]{:S(2)}) collective-permute-start(f32[4,16,1024]{2,1,0:T(8,128)S(1)} %pad_maximum_fusion.rest_0_), channel_id=1, source_target_pairs={{0,3},{1,2},{2,1},{3,0},{4,7},{5,6},{6,5},{7,4},{8,11},{9,10},{10,... | collective-permute-start | bytes 786440 | tf_op jit(solution)/shard_map/ppermute | solution.py:200
  17.7 33.8 %collective-permute-start.4 = (f32[4,16,1024]{2,1,0:T(8,128)S(1)}, f32[4,16,1024]{2,1,0:T(8,128)S(1)}, u32[]{:S(2)}, u32[]{:S(2)}) collective-permute-start(f32[4,16,1024]{2,1,0:T(8,128)S(1)} %pad_maximum_fusion.rest_0_), channel_id=1, source_target_pairs={{0,2},{1,3},{2,0},{3,1},{4,6},{5,7},{6,4},{7,5},{8,10},{9,11},{10,... | collective-permute-start | bytes 786440 | tf_op jit(solution)/shard_map/ppermute | solution.py:200
  18.9 32.6 %collective-permute-start.3 = (f32[4,16,1024]{2,1,0:T(8,128)S(1)}, f32[4,16,1024]{2,1,0:T(8,128)S(1)}, u32[]{:S(2)}, u32[]{:S(2)}) collective-permute-start(f32[4,16,1024]{2,1,0:T(8,128)S(1)} %pad_maximum_fusion.rest_0_), channel_id=1, source_target_pairs={{0,1},{1,0},{2,3},{3,2},{4,5},{5,4},{6,7},{7,6},{8,9},{9,8},{10,11... | collective-permute-start | bytes 786440 | tf_op jit(solution)/shard_map/ppermute | solution.py:200
  19.8 5.2 %collective-permute-start.6 = (f32[4,8192]{1,0:T(4,128)S(1)}, f32[4,8192]{1,0:T(4,128)S(1)}, u32[]{:S(2)}, u32[]{:S(2)}) collective-permute-start(f32[4,8192]{1,0:T(4,128)S(1)} %pad_maximum_fusion.1.rest_4_), channel_id=1, source_target_pairs={{0,16},{16,0},{1,17},{17,1},{2,18},{18,2},{3,19},{19,3},{4,20},{20... | collective-permute-start | bytes 393224 | tf_op jit(solution)/shard_map/ppermute | solution.py:205
  64.4 2.0 %copy-start = (f32[2048,512]{1,0:T(8,128)}, f32[2048,512]{1,0:T(8,128)S(1)}, u32[]{:S(2)}) copy-start(f32[2048,512]{1,0:T(8,128)S(1)} %front_less_update.1.base) | copy-start | bytes 12582916
  109.0 2.2 %copy-start.1 = (f32[2048,512]{1,0:T(8,128)S(1)}, f32[2048,512]{1,0:T(8,128)}, u32[]{:S(2)}) copy-start(f32[2048,512]{1,0:T(8,128)} %copy-done) | copy-start | bytes 12582916
